TPU v7x, 128 devices: a whole 4x4x4 slice. The times are simulated.
128 devices in a mesh: front: 16 (over x, z), grp: 8 (over y, core).
Axes of the slice: x: 4, y: 4, z: 4, core: 2. Of those that a mesh axis runs over, the one named last changes fastest.
Arguments:
- front_block: float32 [16, 16384, 1408], P('front', 'grp'), as said below
- child_blocks: float32 [16, 8, 4, 16, 1408], P('front', 'grp'), may hold values from -0.5 to 0.5
- child_rows: int32 [16, 8, 4, 16], P('front', 'grp'), may hold values from 0 to 2047
- child_dest: int32 [16, 8, 4, 1], P('front', 'grp'), may hold values from 0 to 15; in each aligned block of 4 rows (0 to 3, 4 to 7, ..., all dimensions but the last counted through in order) at most 2 rows name the same one
- panel_owner: int32 [16], P('front'), may hold values from 0 to 7
Outputs:
- panel_factor: float32 [16, 16384, 512], P('front', 'grp')
- schur_block: float32 [16, 16384, 896], P('front', 'grp')
Inputs may be any that keep to these rules, and one draw needn't show every extreme that they name: `child_dest`: among the 4 blocks of one device no front is named more than 2 times, and in every draw some device names some front exactly 2 times. `front_block`: for every front and row block, the first 512 rows' leading 512 x 512 block has a positive diagonal that dominates; other entries lie within -2.3 to 2.3.
All inputs are finite; a program needn't handle non-finite values.
Results may differ from a plain program's by a relative error of at most 0.0003.
Values sent between devices are 32-bit elements; how exact they have to be, the bound alone decides.
A program may use at most 128 MiB of HBM per device.

v0:
```python
import jax
import jax.numpy as jnp
from jax import lax
from jax.sharding import PartitionSpec as P

PB = 512
CAP = 2


def spread(array, axis, root):
    mine = lax.axis_index(axis) == root
    return lax.psum(jnp.where(mine, array, jnp.zeros_like(array)), axis)


def right_solve(factor, rows):
    return lax.linalg.triangular_solve(factor, rows, left_side=False, lower=True, transpose_a=True)


def pack_slots(values, slot_index, front_count):
    empty = jnp.zeros((front_count * CAP,) + values.shape[1:], values.dtype)
    filled = empty.at[slot_index].set(values)
    return filled.reshape((front_count, CAP) + values.shape[1:])


def local(front_block, child_blocks, child_rows, child_dest, panel_owner):
    local_rows = front_block[0]
    front_count = lax.axis_size("front")
    blocks = child_blocks[0, 0]
    row_lists = child_rows[0, 0]
    target_front = child_dest[0, 0, :, 0]
    block_count = target_front.shape[0]
    position = jnp.arange(block_count, dtype=jnp.int32)
    same_front = target_front[:, None] == target_front[None, :]
    earlier = position[None, :] < position[:, None]
    slot_index = target_front * CAP + jnp.sum((same_front & earlier).astype(jnp.int32), axis=1)
    send_rows = pack_slots(row_lists, slot_index, front_count)
    panel_cols = PB
    send_blocks = pack_slots(blocks, slot_index, front_count)
    got_blocks, got_rows = (
        lax.all_to_all(send_blocks, "front", split_axis=0, concat_axis=0, tiled=True),
        lax.all_to_all(send_rows, "front", split_axis=0, concat_axis=0, tiled=True),
    )
    flat_rows = got_rows.reshape(-1)
    local_rows = local_rows.at[flat_rows].add(got_blocks.reshape(-1, local_rows.shape[1]))
    win_cols = local_rows.shape[1] - panel_cols
    owner_index = panel_owner[0]
    is_owner = lax.axis_index("grp") == owner_index
    pivot_block = spread(local_rows[:panel_cols, :panel_cols], "grp", owner_index)
    symmetric = 0.5 * (pivot_block + pivot_block.T)
    pivot_factor = jnp.linalg.cholesky(symmetric)
    solved = right_solve(pivot_factor, local_rows[:, :panel_cols])
    window = spread(solved[panel_cols : panel_cols + win_cols], "grp", owner_index)
    schur_part = local_rows[:, panel_cols:] - jnp.dot(
        solved, window.T, precision=lax.Precision.HIGHEST
    )
    top_rows = jnp.where(is_owner, pivot_factor, solved[:panel_cols])
    panel_rows = jnp.concatenate([top_rows, solved[panel_cols:]], axis=0)
    return (panel_rows[None], schur_part[None])


def solution(mesh):
    placed = (
        P("front", "grp", None),
        P("front", "grp", None, None, None),
        P("front", "grp", None, None),
        P("front", "grp", None, None),
        P("front"),
    )
    return jax.shard_map(
        local,
        mesh=mesh,
        in_specs=placed,
        out_specs=(P("front", "grp", None), P("front", "grp", None)),
        check_vma=False,
    )
```

profile of v0, /device:TPU:0, one launch (start us, length us, event | category | flops | bytes accessed | tf_op | source)
XLA Modules:
  0.0 405.6 jit_solution(12922909138778709445)
XLA Ops:
  7.2 9.4 %copy.71 = f32[1,2048,1408]{2,1,0:T(8,128)} copy(f32[1,2048,1408]{2,1,0:T(8,128)} %param.5) | data formatting | bytes 23068672
  16.8 1.2 scatter_custom_fusion
  18.0 8.0 %all-to-all-start = ((s32[16,2,16]{2,1,0:T(2,128)}), s32[16,2,16]{2,1,0:T(2,128)S(1)}, u32[]{:S(2)}, u32[]{:S(2)}) async-start(s32[16,2,16]{2,1,0:T(2,128)} %bitcast.7), calls=%async_computation | async-start | bytes 32768 | tf_op jit(solution)/shard_map/all_to_all | solution.py:41
  26.0 1.8 broadcast_in_dim.26
  27.7 2.3 scatter_fusion
  30.1 3.5 all-to-all-done
  33.6 3.7 all-to-all-start.1
  38.1 38.4 %all-to-all-done.1 = f32[16,2,16,1408]{3,2,1,0:T(8,128)S(1)} async-done(((f32[16,2,16,1408]{3,2,1,0:T(8,128)}), f32[16,2,16,1408]{3,2,1,0:T(8,128)S(1)}, u32[]{:S(2)}, u32[]{:S(2)}) %all-to-all-start.1) | async-done | bytes 2883616 | tf_op jit(solution)/shard_map/all_to_all | solution.py:40
  76.6 14.0 %scatter_fusion.1 = f32[2048,1408]{1,0:T(8,128)} fusion(f32[2048,1408]{1,0:T(8,128)} %bitcast.75, s32[512]{0:T(512)S(1)} %bitcast.78, f32[512,1408]{1,0:T(8,128)S(1)} %bitcast.76), kind=kCustom, calls=%fused_computation.2 | custom fusion | flops 720896 | bytes 8652800 | tf_op jit(solution)/shard_map/scatter-add | solution.py:44
  90.6 1.3 slice.139
  91.9 0.3 copy.48
  92.2 1.1 broadcast_select_fusion
  93.6 60.5 %all-reduce.4.cloned.1.call-done = f32[512,512]{0,1:T(8,128)} async-done(((f32[512,512]{0,1:T(8,128)}), f32[512,512]{0,1:T(8,128)}) %all-reduce.4.cloned.1.call-update) | async-done | bytes 1048592 | tf_op jit(solution)/shard_map/psum | solution.py:12
  154.1 1.6 copy.34
  155.6 1.5 fusion.16
  157.1 0.3 copy.35
  157.5 0.2 fusion.15
  157.7 11.7 %cholesky.103 = f32[128,128]{1,0:T(8,128)S(1)} custom-call(f32[128,128]{1,0:T(8,128)S(1)} %cholesky.263), custom_call_target="Cholesky" | custom-call | tf_op jit(solution)/shard_map/jit(cholesky)/cholesky | solution.py:50
  169.5 9.8 %custom-call.30 = f32[1,128,128]{1,2,0:T(8,128)S(1)} custom-call(f32[1,128,128]{2,1,0:T(8,128)S(1)} %get-tuple-element.43), custom_call_target="InvertDiagBlocksLowerTriangular" | custom-call | tf_op jit(solution)/shard_map/jit(cholesky)/cholesky | solution.py:50
  179.3 0.3 fusion.21
  179.6 0.3 convolution_subtract_fusion.2
  179.9 11.7 %cholesky.215 = f32[128,128]{1,0:T(8,128)S(1)} custom-call(f32[128,128]{1,0:T(8,128)S(1)} %cholesky.267), custom_call_target="Cholesky" | custom-call | tf_op jit(solution)/shard_map/jit(cholesky)/cholesky | solution.py:50
  192.2 10.2 %custom-call.31 = f32[1,128,128]{1,2,0:T(8,128)S(1)} custom-call(f32[1,128,128]{2,1,0:T(8,128)S(1)} %get-tuple-element.41), custom_call_target="InvertDiagBlocksLowerTriangular" | custom-call | tf_op jit(solution)/shard_map/jit(cholesky)/cholesky | solution.py:50
  202.4 0.3 convolution_dynamic-update-slice_fusion
  202.7 0.6 convolution_subtract_fusion.3
  203.3 11.7 %cholesky.236 = f32[128,128]{1,0:T(8,128)S(1)} custom-call(f32[128,128]{1,0:T(8,128)S(1)} %cholesky.272), custom_call_target="Cholesky" | custom-call | tf_op jit(solution)/shard_map/jit(cholesky)/cholesky | solution.py:50
  215.2 9.8 %custom-call.32 = f32[1,128,128]{1,2,0:T(8,128)S(1)} custom-call(f32[1,128,128]{2,1,0:T(8,128)S(1)} %get-tuple-element.39), custom_call_target="InvertDiagBlocksLowerTriangular" | custom-call | tf_op jit(solution)/shard_map/jit(cholesky)/cholesky | solution.py:50
  225.0 0.3 convolution_dynamic-update-slice_fusion.1
  225.3 0.5 convolution_subtract_fusion.4
  225.8 11.9 %cholesky.253 = f32[128,128]{1,0:T(8,128)S(1)} custom-call(f32[128,128]{1,0:T(8,128)S(1)} %convolution_subtract_fusion.4), custom_call_target="Cholesky" | custom-call | tf_op jit(solution)/shard_map/jit(cholesky)/cholesky | solution.py:50
  237.8 0.7 compare_reduce_fusion.1
  238.5 0.7 compare_reduce_fusion
  239.2 0.8 compare_reduce_fusion.2
  242.7 10.8 %while.1 = (s32[]{:T(128)}, f32[512,512]{0,1:T(8,128)S(1)}, s32[4,2]{0,1:T(2,128)S(1)}, f32[4,128,128]{2,1,0:T(8,128)}, s32[]{:T(128)}) while((s32[]{:T(128)}, f32[512,512]{0,1:T(8,128)S(1)}, s32[4,2]{0,1:T(2,128)S(1)}, f32[4,128,128]{2,1,0:T(8,128)}, s32[]{:T(128)}) %tuple.33), condition=%wide.while_cond, body=%wide.while_body.sunk | while | flops 2 | bytes 393829 | solution.py:16
  242.7 0.5 fusion.50
  243.3 1.3 dynamic-slice.7
  244.7 0.6 bitcast_dynamic-update-slice_fusion.2
  245.4 0.5 fusion.50
  246.0 1.3 dynamic-slice.7
  247.4 0.6 bitcast_dynamic-update-slice_fusion.2
  248.1 0.5 fusion.50
  248.7 1.3 dynamic-slice.7
  250.1 0.6 bitcast_dynamic-update-slice_fusion.2
  250.8 0.5 fusion.50
  251.4 1.3 dynamic-slice.7
  252.8 0.6 bitcast_dynamic-update-slice_fusion.2
  253.4 40.2 %custom-call.33 = f32[4,128,128]{1,2,0:T(8,128)S(1)} custom-call(f32[4,128,128]{2,1,0:T(8,128)} %get-tuple-element.9), custom_call_target="InvertDiagBlocksLowerTriangular" | custom-call | tf_op jit(solution)/shard_map/triangular_solve | solution.py:16
  293.6 2.3 fusion.13
  295.9 3.0 convolution_subtract_fusion.1
  299.0 1.1 fusion.28
  300.1 4.8 %convolution_subtract_fusion = f32[2048,128]{1,0:T(8,128)S(1)} fusion(f32[2048,128]{0,1:T(8,128)S(1)} %fusion.28, f32[2048,128]{0,1:T(8,128)S(1)} %fusion.13, f32[2048,1408]{1,0:T(8,128)} %scatter_fusion.1, f32[512,512]{0,1:T(8,128)S(1)} %get-tuple-element.98), kind=kOutput, calls=%fused_computation.16 | convolution fusion | flops 806092800 | bytes 4325376 | tf_op jit(solution)/shard_map/triangular_solve | solution.py:16
  304.9 1.1 fusion.27
  306.0 7.0 %fusion.7 = f32[2048,128]{1,0:T(8,128)S(1)} fusion(f32[2048,128]{0,1:T(8,128)S(1)} %fusion.27, f32[2048,128]{0,1:T(8,128)S(1)} %fusion.28, f32[2048,128]{0,1:T(8,128)S(1)} %fusion.13, f32[2048,1408]{1,0:T(8,128)} %scatter_fusion.1, f32[512,512]{0,1:T(8,128)} %copy-done.6), kind=kOutput, calls=%fused_computation.15 | convolution fusion | flops 1209794560 | bytes 5439488 | tf_op jit(solution)/shard_map/triangular_solve | solution.py:16
  313.0 1.1 fusion.26
  314.1 1.0 copy-done.2
  315.1 1.4 maximum_select_fusion
  316.6 1.7 pad_maximum_fusion
  318.3 0.3 slice.140
  318.6 0.9 copy-done.3
  319.5 0.3 copy-done.5
  320.1 2.4 maximum_bitcast_fusion
  322.4 5.4 %copy.44 = f32[1,2048,512]{2,1,0:T(8,128)} copy(f32[1,2048,512]{1,2,0:T(8,128)} %maximum_bitcast_fusion) | data formatting | bytes 8388608
  327.8 53.1 %all-reduce.6.cloned.1.call-done = f32[896,512]{0,1:T(8,128)} async-done(((f32[896,512]{0,1:T(8,128)}), f32[896,512]{0,1:T(8,128)}) %all-reduce.6.cloned.1.call-update) | async-done | bytes 1835024 | tf_op jit(solution)/shard_map/psum | solution.py:12
  380.9 17.7 %fusion = f32[1,2048,896]{2,1,0:T(8,128)} fusion(f32[2048,1408]{1,0:T(8,128)} %scatter_fusion.1, f32[896,512]{0,1:T(8,128)} %all-reduce.6.cloned.1.call-done, f32[2048,128]{0,1:T(8,128)} %copy-done.2, f32[2048,128]{0,1:T(8,128)S(1)} %fusion.27, f32[2048,128]{0,1:T(8,128)S(1)} %fusion.28, f32[2048,128]{0,1:T(8,128)S(1)} %fusion.13), kind=kOutput, calls=%fused_computation.6 | convolution fusion | flops 11279269888 | bytes 20709376 | tf_op jit(solution)/shard_map/dot_general | solution.py:53
  (53 shorter events, 2.4 us)
Async XLA Ops:
  7.2 9.7 %copy-start = (s32[1,1,4,16]{3,2,1,0:T(4,128)S(1)}, s32[1,1,4,16]{3,2,1,0:T(4,128)}, u32[]{:S(2)}) copy-start(s32[1,1,4,16]{3,2,1,0:T(4,128)} %param.7) | copy-start | bytes 772
  7.2 20.6 %copy-start.7 = (f32[1,1,4,16,1408]{4,3,2,1,0:T(8,128)S(1)}, f32[1,1,4,16,1408]{4,3,2,1,0:T(8,128)}, u32[]{:S(2)}) copy-start(f32[1,1,4,16,1408]{4,3,2,1,0:T(8,128)} %param.6) | copy-start | bytes 1081348
  7.2 9.4 %copy-start.8 = (s32[1,1,4,1]{2,3,1,0:T(1,128)S(1)}, s32[1,1,4,1]{2,3,1,0:T(1,128)}, u32[]{:S(2)}) copy-start(s32[1,1,4,1]{2,3,1,0:T(1,128)} %param.8) | copy-start | bytes 52
  18.0 15.6 %all-to-all-start = ((s32[16,2,16]{2,1,0:T(2,128)}), s32[16,2,16]{2,1,0:T(2,128)S(1)}, u32[]{:S(2)}, u32[]{:S(2)}) async-start(s32[16,2,16]{2,1,0:T(2,128)} %bitcast.7), calls=%async_computation | async-start | bytes 32768 | tf_op jit(solution)/shard_map/all_to_all | solution.py:41
  33.6 43.0 %all-to-all-start.1 = ((f32[16,2,16,1408]{3,2,1,0:T(8,128)}), f32[16,2,16,1408]{3,2,1,0:T(8,128)S(1)}, u32[]{:S(2)}, u32[]{:S(2)}) async-start(f32[16,2,16,1408]{3,2,1,0:T(8,128)} %bitcast.10), calls=%async_computation.1 | async-start | bytes 5767168 | tf_op jit(solution)/shard_map/all_to_all | solution.py:40
  37.3 116.8 %all-reduce.4.cloned.1.call-start = ((), (), s32[]{:S(2)}) async-start(), calls=%async_computation.2 | async-start | bytes 2097152 | tf_op jit(solution)/shard_map/psum | solution.py:12
  93.3 287.6 %all-reduce.6.cloned.1.call-start = ((), (), s32[]{:S(2)}) async-start(), calls=%async_computation.3 | async-start | bytes 3670016 | tf_op jit(solution)/shard_map/psum | solution.py:12
  239.2 14.3 %copy-start.4 = (f32[512,512]{0,1:T(8,128)}, f32[512,512]{0,1:T(8,128)S(1)}, u32[]{:S(2)}) copy-start(f32[512,512]{0,1:T(8,128)S(1)} %constant_dynamic-update-slice_fusion.1) | copy-start | bytes 3145732
  253.4 46.6 %copy-start.6 = (f32[512,512]{0,1:T(8,128)}, f32[512,512]{0,1:T(8,128)S(1)}, u32[]{:S(2)}) copy-start(f32[512,512]{0,1:T(8,128)S(1)} %get-tuple-element.98) | copy-start | bytes 3145732
  314.1 1.0 copy-start.2
  318.3 1.2 copy-start.3
  318.3 1.5 copy-start.5
  380.9 17.7 %copy-start.1 = (s32[1,1,4,16]{3,2,1,0:T(4,128)S(1)}, s32[1,1,4,16]{3,2,1,0:T(4,128)}, u32[]{:S(2)}) copy-start(s32[1,1,4,16]{3,2,1,0:T(4,128)} %param.7) | copy-start | bytes 772
Sparse Core Ops, SparseCore 0:
  93.4 60.5 all-reduce.3
  316.7 64.1 all-reduce.5
where the time goes:
time: 412 us; the launch traced here: 406 us
  waiting for transfers between devices  156 us (38%)
  other arithmetic  142 us (34%)
  matrix products  40.4 us (10%)
  local copies, waits for them, and re-layouts  37.6 us (9%)
  between operations  17.9 us (4%)
  starting transfers between devices  12 us (3%)
    psum x2, waiting for transfers between devices, spread(): return lax.psum(jnp.where(mine, array, jnp.zeros_like(array)), axis)  114 us
    another operation x14, other arithmetic, local(): pivot_factor = jnp.linalg.cholesky(symmetric)  79.1 us
    another operation x4, other arithmetic, right_solve(): lax.linalg.triangular_solve(factor, rows, left_side=False, lower=True, tr...  42 us
    all_to_all x1, waiting for transfers between devices, local(): lax.all_to_all(send_blocks, 'front', split_axis=0, concat_axis=0, tiled=T...  38.4 us
    another operation x7, matrix products, right_solve(): lax.linalg.triangular_solve(factor, rows, left_side=False, lower=True, tr...  20.5 us
    dot_general x1, matrix products, local(): jnp.dot(solved, window.T, precision=lax.Precision.HIGHEST)  17.7 us
    unnamed x21, local copies, waits for them, and re-layouts  17.4 us
    scatter-add x1, other arithmetic, local(): local_rows.at[flat_rows].add(got_blocks.reshape(-1, local_rows.shape[1]))  14 us
  transfers between devices with their start and end apart: 4, of which 4 were waited for; matrix products, arithmetic and copies ran while one was open for 3% of the time, Pallas kernels for 0%

commit v1 on v0

v1 whole, which is shorter than its diff:
```python
import functools

import jax
import jax.numpy as jnp
from jax import lax
from jax.experimental import pallas as pl
from jax.experimental.pallas import tpu as pltpu
from jax.sharding import PartitionSpec as P

F32, BF16 = jnp.float32, jnp.bfloat16
MESH = pl.DeviceIdType.MESH
PB, WIN, KB, BR, CAP = 512, 896, 4, 16, 2
NFRONT, NCHIP = 16, 4
SLOT = CAP * BR
KALL = NFRONT * SLOT
NB = 128
STEPS = PB // NB
SB = 16
CHUNKS = 7
PIECE = WIN // (4 * CHUNKS)
TURNS = CHUNKS + 3

NN = (((1,), (0,)), ((), ()))
NT = (((1,), (1,)), ((), ()))
TN = (((0,), (0,)), ((), ()))


def split(x):
    high = x.astype(BF16).astype(F32)
    return high, x - high


def dot(a, b, dims):
    return lax.dot_general(a.astype(BF16), b.astype(BF16), dims, preferred_element_type=F32)


def dot3(a, b, dims):
    ah, al = split(a)
    bh, bl = split(b)
    return dot(ah, bh, dims) + (dot(ah, bl, dims) + dot(al, bh, dims))


def eliminate(d_ref, k):
    n, b, c0 = NB, SB, k * SB
    lane = lax.broadcasted_iota(jnp.int32, (1, n), 1)
    rows = [d_ref[pl.ds(c0 + i, 1), :] for i in range(b)]
    s = [[None] * b for _ in range(b)]
    for j in range(b):
        for i in range(j, b):
            s[i][j] = jnp.broadcast_to(rows[j][:, c0 + i : c0 + i + 1], (1, n))
    inside = (lane >= c0) & (lane < c0 + b)
    rows = [jnp.where(inside, jnp.where(lane == c0 + i, 1.0, 0.0), rows[i]) for i in range(b)]
    for j in range(b):
        inv = lax.rsqrt(s[j][j])
        for i in range(j + 1, b):
            s[i][j] = s[i][j] * inv
        rows[j] = rows[j] * inv
        for i in range(j + 1, b):
            for q in range(j + 1, i + 1):
                s[i][q] = s[i][q] - s[i][j] * s[q][j]
        for i in range(j + 1, b):
            rows[i] = rows[i] - s[i][j] * rows[j]
        d_ref[pl.ds(c0 + j, 1), :] = rows[j]
    if c0 + b < n:
        u = d_ref[pl.ds(c0, b), :]
        col = lax.broadcasted_iota(jnp.int32, (b, n), 1)
        left = jnp.where(col >= c0 + b, u, 0.0)
        uh, ul = split(u)
        lh, ll = split(left)
        update = dot(jnp.concatenate([lh, lh, ll], 0), jnp.concatenate([uh, ul, uh], 0), TN)
        below = n - c0 - b
        old = d_ref[pl.ds(c0 + b, below), :]
        col = lax.broadcasted_iota(jnp.int32, (below, n), 1)
        old = jnp.where((col >= c0) & (col < c0 + b), 0.0, old)
        d_ref[pl.ds(c0 + b, below), :] = old - update[c0 + b :, :]


def gather_kernel(
    front_ref, blocks_ref, rows_ref, dest_ref, owner_ref,
    win_out, w_out, sym_out, panel_out, trail_out, index_out,
    part, rowbuf, send_p, send_t, send_i, got_p, got_t, got_i,
    table, diag, pre_win, ring_in, ring_out, pair_in,
    pre_w, chip_w, far_w, half_w, pair_w,
    load_sem, own_sem, xs_sem, xr_sem, pw_sem, rs_sem, rr_sem, ps_sem, pr_sem,
    qs_sem, qr_sem, fs_sem, fr_sem, hs_sem, hr_sem,
):
    front = lax.axis_index("front")
    group = lax.axis_index("grp")
    chip, core = group // 2, group % 2
    rest = PB + WIN

    load = pltpu.make_async_copy(front_ref.at[0, pl.ds(0, rest), pl.ds(0, PB)], part, load_sem)
    load.start()

    barrier = pltpu.get_barrier_semaphore()

    def greet(step, carry):
        pl.semaphore_signal(barrier, inc=1, device_id={"front": lax.rem(front + step, NFRONT)}, device_id_type=MESH)
        return carry

    lax.fori_loop(1, NFRONT, greet, 0)
    partner = 2 * chip + (1 - core)
    pl.semaphore_signal(barrier, inc=1, device_id={"grp": partner}, device_id_type=MESH)
    for step in range(1, NCHIP):
        there = 2 * lax.rem(chip + step, NCHIP) + core
        pl.semaphore_signal(barrier, inc=1, device_id={"grp": there}, device_id_type=MESH)

    rowbuf[...] = jnp.zeros_like(rowbuf)
    rowbuf[0:KB, 0:BR] = rows_ref[...]
    spread = rowbuf[...]
    for width in (16, 32, 64):
        spread = spread + pltpu.roll(spread, width, 1)
    rowbuf[...] = spread
    dests = [dest_ref[k] for k in range(KB)]
    ranks = []
    for k in range(KB):
        rank = jnp.int32(0)
        for e in range(k):
            rank = rank + (dests[e] == dests[k]).astype(jnp.int32)
        ranks.append(rank)
    lane = lax.broadcasted_iota(jnp.int32, (8, 128), 1)
    mine = lax.rem(front, 4) * SLOT

    def choose(to, slot):
        pick, found = jnp.int32(0), jnp.int32(0)
        for k in range(KB):
            hit = ((dests[k] == to) & (ranks[k] == slot)).astype(jnp.int32)
            pick = pick + hit * k
            found = found + hit
        return pick, found

    def pack_panel(to, carry):
        index = jnp.zeros((8, 128), jnp.int32)
        for slot in range(CAP):
            pick, found = choose(to, slot)
            send_p[to, slot * BR : (slot + 1) * BR, :] = blocks_ref[pick, :, 0:PB]
            at = jnp.broadcast_to(rowbuf[pl.ds(pick, 1), :], (8, 128))
            at = jnp.where(found > 0, at, -1)
            base = mine + slot * BR
            index = jnp.where((lane >= base) & (lane < base + BR), at, index)
        send_i[to] = index
        return carry

    lax.fori_loop(0, NFRONT, pack_panel, 0)
    pl.semaphore_wait(barrier, NFRONT - 1 + 1 + NCHIP - 1)

    def exchange(src, dst, kind, step):
        to = lax.rem(front + step, NFRONT)
        return pltpu.make_async_remote_copy(
            src_ref=src.at[to], dst_ref=dst.at[front],
            send_sem=xs_sem.at[kind, step], recv_sem=xr_sem.at[kind, step],
            device_id={"front": to}, device_id_type=MESH,
        )

    def arrival(src, dst, kind, step):
        came = lax.rem(front + NFRONT - step, NFRONT)
        return pltpu.make_async_remote_copy(
            src_ref=src.at[came], dst_ref=dst.at[came],
            send_sem=xs_sem.at[kind, step], recv_sem=xr_sem.at[kind, step],
            device_id={"front": came}, device_id_type=MESH,
        )

    def send_first(step, carry):
        exchange(send_i, got_i, 0, step).start()
        exchange(send_p, got_p, 1, step).start()
        return carry

    lax.fori_loop(1, NFRONT, send_first, 0)
    own_i = pltpu.make_async_copy(send_i.at[front], got_i.at[front], own_sem.at[0])
    own_p = pltpu.make_async_copy(send_p.at[front], got_p.at[front], own_sem.at[1])
    own_i.start()
    own_p.start()

    def pack_trail(to, carry):
        for slot in range(CAP):
            pick, _ = choose(to, slot)
            send_t[to, slot * BR : (slot + 1) * BR, :] = blocks_ref[pick, :, PB:]
        return carry

    lax.fori_loop(0, NFRONT, pack_trail, 0)

    def send_second(step, carry):
        exchange(send_t, got_t, 2, step).start()
        return carry

    lax.fori_loop(1, NFRONT, send_second, 0)
    own_t = pltpu.make_async_copy(send_t.at[front], got_t.at[front], own_sem.at[2])
    own_t.start()

    load.wait()
    own_i.wait()
    own_p.wait()

    def take_first(step, carry):
        arrival(send_i, got_i, 0, step).wait_recv()
        arrival(send_p, got_p, 1, step).wait_recv()
        return carry

    lax.fori_loop(1, NFRONT, take_first, 0)

    pieces = []
    for q in range(NFRONT // 4):
        piece = got_i[4 * q, 0:1, :]
        for s in range(1, 4):
            piece = piece + got_i[4 * q + s, 0:1, :]
        pieces.append(piece)
    index = jnp.concatenate(pieces, axis=1)
    index_out[...] = jnp.broadcast_to(index, (8, KALL))
    child = got_p[...].reshape(KALL, PB)
    panel_out[...] = child
    high, low = split(child)
    high, low = high.astype(BF16), low.astype(BF16)

    def assemble(tile, carry):
        base = pl.multiple_of(tile * NB, NB)
        at = lax.broadcasted_iota(jnp.int32, (NB, KALL), 0) + base
        onehot = jnp.where(at == index, 1.0, 0.0).astype(BF16)
        add = dot(onehot, high, NN) + dot(onehot, low, NN)
        part[pl.ds(base, NB), :] = part[pl.ds(base, NB), :] + add
        return carry

    lax.fori_loop(0, rest // NB, assemble, 0)

    half = WIN // 2
    give = pltpu.make_async_remote_copy(
        src_ref=part.at[pl.ds(PB + (1 - core) * half, half), :], dst_ref=pre_win,
        send_sem=pw_sem.at[0], recv_sem=pw_sem.at[1], device_id={"grp": partner}, device_id_type=MESH,
    )
    give.start()

    pivot = part[0:PB, :]
    sym = 0.5 * (pivot + pivot.T)
    sym_out[...] = sym
    table[...] = sym

    owner = owner_ref[0]
    owner_chip = owner // 2
    own_me = owner == group
    own_pair = owner == partner
    shift_right = lax.rem(chip - owner_chip + NCHIP, NCHIP)
    shift_left = lax.rem(owner_chip - chip + NCHIP, NCHIP)

    def ring(way, turn):
        to = 2 * lax.rem(chip + (1 if way == 0 else NCHIP - 1), NCHIP) + core
        return pltpu.make_async_remote_copy(
            src_ref=ring_out.at[way, turn], dst_ref=ring_in.at[way, turn],
            send_sem=rs_sem.at[way, turn], recv_sem=rr_sem.at[way, turn],
            device_id={"grp": to}, device_id_type=MESH,
        )

    def pair(way, turn):
        return pltpu.make_async_remote_copy(
            src_ref=ring_out.at[way, turn], dst_ref=pair_in.at[way, turn],
            send_sem=ps_sem.at[way, turn], recv_sem=pr_sem.at[way, turn],
            device_id={"grp": partner}, device_id_type=MESH,
        )

    def window_turn(turn):
        if turn == 0:
            give.wait_recv()
        for way in range(2):
            if turn > 0:
                ring(way, turn - 1).wait_recv()
            if turn < CHUNKS:
                at = way * (half // 2) + turn * PIECE
                value = part[pl.ds(PB + core * half + at, PIECE), :]
                value = jnp.where(own_me, value, pre_win[pl.ds(at, PIECE), :])
                if turn > 0:
                    value = jnp.where(own_me | own_pair, value, ring_in[way, turn - 1])
            else:
                value = ring_in[way, turn - 1]
            ring_out[way, turn] = value
            if turn < TURNS - 1:
                ring(way, turn).start()
            pair(way, turn).start()

    def width(k):
        return NB * (k + 1)

    def pair_rows(k):
        return pltpu.make_async_remote_copy(
            src_ref=table.at[pl.ds(k * NB + (1 - core) * (NB // 2), NB // 2), pl.ds(0, width(k))],
            dst_ref=pre_w.at[k, :, pl.ds(0, width(k))],
            send_sem=qs_sem.at[k], recv_sem=qr_sem.at[k], device_id={"grp": partner}, device_id_type=MESH,
        )

    def far_rows(k, step):
        to = 2 * lax.rem(chip + step, NCHIP) + core
        return pltpu.make_async_remote_copy(
            src_ref=chip_w.at[k, :, pl.ds(0, width(k))], dst_ref=far_w.at[step - 1, k, :, pl.ds(0, width(k))],
            send_sem=fs_sem.at[step - 1, k], recv_sem=fr_sem.at[step - 1, k],
            device_id={"grp": to}, device_id_type=MESH,
        )

    def back_rows(k):
        return pltpu.make_async_remote_copy(
            src_ref=half_w.at[k, :, pl.ds(0, width(k))], dst_ref=pair_w.at[k, :, pl.ds(0, width(k))],
            send_sem=hs_sem.at[k], recv_sem=hr_sem.at[k], device_id={"grp": partner}, device_id_type=MESH,
        )

    def spread_a(k):
        pair_rows(k).start()

    def spread_b(k):
        pair_rows(k).wait_recv()
        cols = pl.ds(0, width(k))
        own = table[pl.ds(k * NB + core * (NB // 2), NB // 2), cols]
        chip_w[k, :, cols] = jnp.where(own_me, own, pre_w[k, :, cols])
        for step in range(1, NCHIP):
            far_rows(k, step).start()

    def spread_c(k):
        cols = pl.ds(0, width(k))
        value = chip_w[k, :, cols]
        for step in range(1, NCHIP):
            far_rows(k, step).wait_recv()
            value = jnp.where(shift_right == step, far_w[step - 1, k, :, cols], value)
        half_w[k, :, cols] = value
        back_rows(k).start()
        w_out[pl.ds(k * NB + core * (NB // 2), NB // 2), cols] = value

    def spread_d(k):
        back_rows(k).wait_recv()
        cols = pl.ds(0, width(k))
        w_out[pl.ds(k * NB + (1 - core) * (NB // 2), NB // 2), cols] = pair_w[k, :, cols]

    w_out[...] = jnp.zeros_like(w_out)

    def after(k, ib):
        if k == 0 and ib == 1:
            window_turn(0)
        if ib == 5:
            window_turn(2 * k + 1)
        if k > 0 and ib == 1:
            window_turn(2 * k)
            spread_b(k - 1)
        if k > 1 and ib == 3:
            spread_c(k - 2)
        if k > 1 and ib == 7:
            spread_d(k - 2)

    wide = lax.broadcasted_iota(jnp.int32, (NB, PB), 1)
    for k in range(STEPS):
        base = k * NB
        diag[...] = table[base : base + NB, base : base + NB]
        for ib in range(NB // SB):
            eliminate(diag, ib)
            after(k, ib)
        inverse = jnp.where(
            lax.broadcasted_iota(jnp.int32, (NB, NB), 0) >= lax.broadcasted_iota(jnp.int32, (NB, NB), 1),
            diag[...], 0.0,
        )
        above = table[base : base + NB, :]
        above = jnp.where((wide >= base) & (wide < base + NB), 0.0, above)
        reduced = dot3(inverse, above, NN)
        table[base : base + NB, :] = reduced
        table[base : base + NB, base : base + NB] = inverse
        spread_a(k)
        if k + 1 < STEPS:
            upper = table[base : base + NB, :]
            left = reduced[:, base + NB :]
            update = dot3(left, upper, TN)
            old = table[base + NB :, :]
            col = lax.broadcasted_iota(jnp.int32, old.shape, 1)
            old = jnp.where((col >= base) & (col < base + NB), 0.0, old)
            table[base + NB :, :] = old - update

    window_turn(8)
    spread_b(3)
    spread_c(2)
    window_turn(9)
    spread_c(3)
    spread_d(2)

    for way in range(2):
        pair(way, 0).wait_recv()
        shift = shift_right if way == 0 else shift_left
        for turn in range(1, TURNS):
            pair(way, turn).wait_recv()
        for m in range(CHUNKS):
            at = way * (half // 2) + m * PIECE
            own, other = ring_out[way, m], pair_in[way, m]
            for step in range(1, NCHIP):
                own = jnp.where(shift == step, ring_out[way, m + step], own)
                other = jnp.where(shift == step, pair_in[way, m + step], other)
            win_out[pl.ds(core * half + at, PIECE), :] = own
            win_out[pl.ds((1 - core) * half + at, PIECE), :] = other

    own_t.wait()

    def take_second(step, carry):
        arrival(send_t, got_t, 2, step).wait_recv()
        return carry

    lax.fori_loop(1, NFRONT, take_second, 0)
    trail_out[...] = got_t[...].reshape(KALL, WIN)
    spread_d(3)

    def sent(step, carry):
        exchange(send_i, got_i, 0, step).wait_send()
        exchange(send_p, got_p, 1, step).wait_send()
        exchange(send_t, got_t, 2, step).wait_send()
        return carry

    lax.fori_loop(1, NFRONT, sent, 0)
    give.wait_send()
    for way in range(2):
        for turn in range(TURNS):
            if turn < TURNS - 1:
                ring(way, turn).wait_send()
            pair(way, turn).wait_send()
    for k in range(STEPS):
        pair_rows(k).wait_send()
        back_rows(k).wait_send()
        for step in range(1, NCHIP):
            far_rows(k, step).wait_send()


def gather(front_block, blocks, rows, dest, owner):
    vmem = pl.BlockSpec(memory_space=pltpu.VMEM)
    smem = pl.BlockSpec(memory_space=pltpu.SMEM)
    dma = pltpu.SemaphoreType.DMA
    out = [
        jax.ShapeDtypeStruct((WIN, PB), F32),
        jax.ShapeDtypeStruct((PB, PB), F32),
        jax.ShapeDtypeStruct((PB, PB), F32),
        jax.ShapeDtypeStruct((KALL, PB), F32),
        jax.ShapeDtypeStruct((KALL, WIN), F32),
        jax.ShapeDtypeStruct((8, KALL), jnp.int32),
    ]
    return pl.pallas_call(
        gather_kernel,
        out_shape=out,
        in_specs=[pl.BlockSpec(memory_space=pl.ANY), vmem, vmem, smem, smem],
        out_specs=[vmem] * 6,
        scratch_shapes=[
            pltpu.VMEM((PB + WIN, PB), F32),
            pltpu.VMEM((8, 128), jnp.int32),
            pltpu.VMEM((NFRONT, SLOT, PB), F32),
            pltpu.VMEM((NFRONT, SLOT, WIN), F32),
            pltpu.VMEM((NFRONT, 8, 128), jnp.int32),
            pltpu.VMEM((NFRONT, SLOT, PB), F32),
            pltpu.VMEM((NFRONT, SLOT, WIN), F32),
            pltpu.VMEM((NFRONT, 8, 128), jnp.int32),
            pltpu.VMEM((PB, PB), F32),
            pltpu.VMEM((NB, NB), F32),
            pltpu.VMEM((WIN // 2, PB), F32),
            pltpu.VMEM((2, TURNS, PIECE, PB), F32),
            pltpu.VMEM((2, TURNS, PIECE, PB), F32),
            pltpu.VMEM((2, TURNS, PIECE, PB), F32),
            pltpu.VMEM((STEPS, NB // 2, PB), F32),
            pltpu.VMEM((STEPS, NB // 2, PB), F32),
            pltpu.VMEM((NCHIP - 1, STEPS, NB // 2, PB), F32),
            pltpu.VMEM((STEPS, NB // 2, PB), F32),
            pltpu.VMEM((STEPS, NB // 2, PB), F32),
            dma, dma((3,)), dma((3, NFRONT)), dma((3, NFRONT)), dma((2,)),
            dma((2, TURNS)), dma((2, TURNS)), dma((2, TURNS)), dma((2, TURNS)),
            dma((STEPS,)), dma((STEPS,)), dma((NCHIP - 1, STEPS)), dma((NCHIP - 1, STEPS)),
            dma((STEPS,)), dma((STEPS,)),
        ],
        compiler_params=pltpu.CompilerParams(
            collective_id=0, has_side_effects=True, vmem_limit_bytes=56 * 2**20
        ),
        name="gather",
    )(front_block, blocks, rows, dest, owner)


TILE = 256


def finish_kernel(
    owner_ref, a_ref, cp_ref, ct_ref, idx_ref, w_ref, win_ref, sym_ref, panel_ref, schur_ref,
    wh, wl, vh, vl, ph, pw, th, tw,
):
    step = pl.program_id(0)

    @pl.when(step == 0)
    def _():
        high, low = split(w_ref[...])
        wh[...] = high.astype(BF16)
        wl[...] = low.astype(BF16)
        for base in range(0, WIN, 128):
            raw_h, raw_l = split(win_ref[base : base + 128, :])
            solved = dot(raw_h, wh[...], NT) + (dot(raw_h, wl[...], NT) + dot(raw_l, wh[...], NT))
            high, low = split(solved)
            vh[base : base + 128, :] = high.astype(BF16)
            vl[base : base + 128, :] = low.astype(BF16)
        high, low = split(cp_ref[...])
        ph[...] = high.astype(BF16)
        pw[...] = low.astype(BF16)
        high, low = split(ct_ref[...])
        th[...] = high.astype(BF16)
        tw[...] = low.astype(BF16)

    at = lax.broadcasted_iota(jnp.int32, (TILE, KALL), 0) + step * TILE
    onehot = jnp.where(at == idx_ref[0:1, :], 1.0, 0.0).astype(BF16)
    left = a_ref[0, :, 0:PB] + (dot(onehot, ph[...], NN) + dot(onehot, pw[...], NN))
    lh, ll = split(left)
    solved = dot(lh, wh[...], NT) + (dot(lh, wl[...], NT) + dot(ll, wh[...], NT))
    panel_ref[0] = solved
    sh, sl = split(solved)
    right = a_ref[0, :, PB:] + (dot(onehot, th[...], NN) + dot(onehot, tw[...], NN))
    product = dot(sh, vh[...], NT) + (dot(sh, vl[...], NT) + dot(sl, vh[...], NT))
    schur_ref[0] = right - product

    @pl.when((step < PB // TILE) & (owner_ref[0] == owner_ref[1]))
    def _():
        top = pl.multiple_of(step * TILE, TILE)
        gh, gl = split(sym_ref[pl.ds(top, TILE), :])
        factor = dot(gh, wh[...], NT) + (dot(gh, wl[...], NT) + dot(gl, wh[...], NT))
        row = lax.broadcasted_iota(jnp.int32, (TILE, PB), 0) + top
        panel_ref[0] = jnp.where(row >= lax.broadcasted_iota(jnp.int32, (TILE, PB), 1), factor, 0.0)


def finish(owner2, front_block, cp, ct, index, w, window, sym):
    rows = front_block.shape[1]
    smem = pl.BlockSpec(memory_space=pltpu.SMEM)

    def whole(x):
        return pl.BlockSpec(x.shape, lambda i: (0, 0), pipeline_mode=pl.Buffered(1))

    return pl.pallas_call(
        finish_kernel,
        grid=(rows // TILE,),
        out_shape=[jax.ShapeDtypeStruct((1, rows, PB), F32), jax.ShapeDtypeStruct((1, rows, WIN), F32)],
        in_specs=[smem, pl.BlockSpec((1, TILE, PB + WIN), lambda i: (0, i, 0))]
        + [whole(x) for x in (cp, ct, index, w, window, sym)],
        out_specs=[
            pl.BlockSpec((1, TILE, PB), lambda i: (0, i, 0)),
            pl.BlockSpec((1, TILE, WIN), lambda i: (0, i, 0)),
        ],
        scratch_shapes=[
            pltpu.VMEM((PB, PB), BF16), pltpu.VMEM((PB, PB), BF16),
            pltpu.VMEM((WIN, PB), BF16), pltpu.VMEM((WIN, PB), BF16),
            pltpu.VMEM((KALL, PB), BF16), pltpu.VMEM((KALL, PB), BF16),
            pltpu.VMEM((KALL, WIN), BF16), pltpu.VMEM((KALL, WIN), BF16),
        ],
        compiler_params=pltpu.CompilerParams(vmem_limit_bytes=56 * 2**20),
        name="finish",
    )(owner2, front_block, cp, ct, index, w, window, sym)


def local(front_block, child_blocks, child_rows, child_dest, panel_owner):
    window, w, sym, cp, ct, index = gather(
        front_block, child_blocks[0, 0], child_rows[0, 0], child_dest.reshape(KB), panel_owner
    )
    owner2 = jnp.concatenate([panel_owner, lax.axis_index("grp").astype(jnp.int32)[None]])
    return tuple(finish(owner2, front_block, cp, ct, index, w, window, sym))


def solution(mesh):
    placed = (
        P("front", "grp", None),
        P("front", "grp", None, None, None),
        P("front", "grp", None, None),
        P("front", "grp", None, None),
        P("front"),
    )
    return jax.shard_map(
        local,
        mesh=mesh,
        in_specs=placed,
        out_specs=(P("front", "grp", None), P("front", "grp", None)),
        check_vma=False,
    )
```

time: 412 us -> 126 us (0.31)
  the two profiles are of different devices: /device:TPU:0 before, /device:TPU:3 now
where the time goes in v1:
time: 126 us
  Pallas kernels  124 us (98%)
  between operations  1.29 us (1%)
    pallas_call x1, Pallas kernels, gather(): pl.pallas_call(gather_kernel, out_shape=out, in_specs=[pl.BlockSpec(memor...  96.3 us
    pallas_call x1, Pallas kernels, finish(): pl.pallas_call(finish_kernel, grid=(rows // TILE,), out_shape=[jax.ShapeD...  27.8 us

profile of v1, /device:TPU:3, one launch (start us, length us, event | category | flops | bytes accessed | tf_op | source)
XLA Modules:
  0.0 126.0 jit_solution(8881314060627683601)
XLA Ops:
  1.3 0.6 pad_add_fusion.owner_ref
  1.9 96.3 %gather.1 = (f32[896,512]{1,0:T(8,128)}, f32[512,512]{1,0:T(8,128)}, f32[512,512]{1,0:T(8,128)}, f32[512,512]{1,0:T(8,128)}, f32[512,896]{1,0:T(8,128)}, /*index=5*/s32[8,512]{1,0:T(8,128)}) custom-call(f32[1,2048,1408]{2,1,0:T(8,128)} %a_ref.1, f32[4,16,1408]{2,1,0:T(8,128)} %bitcast.4, s32[4,16]{1,0:T(4,128)} %bitcast.5, s32[4]{0:T(128)} %bitcast.6, ...), custom_call_target="tpu_custom_call" | custom-call | tf_op jit(solution)/shard_map/gather/pallas_call | solution.py:431
  98.2 27.8 %finish.1 = (f32[1,2048,512]{2,1,0:T(8,128)}, f32[1,2048,896]{2,1,0:T(8,128)}) custom-call(s32[2]{0:T(128)} %pad_add_fusion.owner_ref, f32[1,2048,1408]{2,1,0:T(8,128)} %a_ref.1, f32[512,512]{1,0:T(8,128)} %get-tuple-element.8.cp_ref, f32[512,896]{1,0:T(8,128)} %get-tuple-element.9.ct_ref, s32[8,512]{1,0:T(8,128)} %get-tuple-element.10.idx_ref, ...), custom_call_target="tpu_custom_call" | custom-call | tf_op jit(solution)/shard_map/finish/pallas_call | solution.py:522

commit v2 on v0

v2 whole, which is shorter than its diff:
```python
import functools

import jax
import jax.numpy as jnp
from jax import lax
from jax.experimental import pallas as pl
from jax.experimental.pallas import tpu as pltpu
from jax.sharding import PartitionSpec as P

F32, BF16 = jnp.float32, jnp.bfloat16
MESH = pl.DeviceIdType.MESH
PB, WIN, KB, BR, CAP = 512, 896, 4, 16, 2
NFRONT, NCHIP = 16, 4
SLOT = CAP * BR
KALL = NFRONT * SLOT
NB = 128
STEPS = PB // NB
SB = 16
HALVES = 2

NN = (((1,), (0,)), ((), ()))
NT = (((1,), (1,)), ((), ()))
TN = (((0,), (0,)), ((), ()))


def split(x):
    high = x.astype(BF16).astype(F32)
    return high, x - high


def dot(a, b, dims):
    return lax.dot_general(a.astype(BF16), b.astype(BF16), dims, preferred_element_type=F32)


def dot3(a, b, dims):
    ah, al = split(a)
    bh, bl = split(b)
    return dot(ah, bh, dims) + (dot(ah, bl, dims) + dot(al, bh, dims))


def eliminate(d_ref, k):
    n, b, c0 = NB, SB, k * SB
    lane = lax.broadcasted_iota(jnp.int32, (1, n), 1)
    rows = [d_ref[pl.ds(c0 + i, 1), :] for i in range(b)]
    s = [[None] * b for _ in range(b)]
    for j in range(b):
        for i in range(j, b):
            s[i][j] = jnp.broadcast_to(rows[j][:, c0 + i : c0 + i + 1], (1, n))
    inside = (lane >= c0) & (lane < c0 + b)
    rows = [jnp.where(inside, jnp.where(lane == c0 + i, 1.0, 0.0), rows[i]) for i in range(b)]
    for j in range(b):
        inv = lax.rsqrt(s[j][j])
        for i in range(j + 1, b):
            s[i][j] = s[i][j] * inv
        rows[j] = rows[j] * inv
        for i in range(j + 1, b):
            for q in range(j + 1, i + 1):
                s[i][q] = s[i][q] - s[i][j] * s[q][j]
        for i in range(j + 1, b):
            rows[i] = rows[i] - s[i][j] * rows[j]
        d_ref[pl.ds(c0 + j, 1), :] = rows[j]
    if c0 + b < n:
        u = d_ref[pl.ds(c0, b), :]
        col = lax.broadcasted_iota(jnp.int32, (b, n), 1)
        left = jnp.where(col >= c0 + b, u, 0.0)
        uh, ul = split(u)
        lh, ll = split(left)
        update = dot(jnp.concatenate([lh, lh, ll], 0), jnp.concatenate([uh, ul, uh], 0), TN)
        below = n - c0 - b
        old = d_ref[pl.ds(c0 + b, below), :]
        col = lax.broadcasted_iota(jnp.int32, (below, n), 1)
        old = jnp.where((col >= c0) & (col < c0 + b), 0.0, old)
        d_ref[pl.ds(c0 + b, below), :] = old - update[c0 + b :, :]


HOPS = [(dx, dz) for dx in range(4) for dz in range(4)][1:]
HOPS.sort(key=lambda p: -(min(p[0], 4 - p[0]) + min(p[1], 4 - p[1])))
TILE_A = 256


class Spread:
    def __init__(self, ids, flags, src, full, base, rows, width, pre, cand, part, sems):
        self.chip, self.core, self.partner = ids
        self.own_me, self.shift = flags
        self.src, self.full, self.base, self.rows, self.width = src, full, base, rows, width
        self.pre, self.cand, self.part, self.sems = pre, cand, part, sems

    def copy(self, src, dst, sem, to):
        return pltpu.make_async_remote_copy(
            src_ref=src, dst_ref=dst, send_sem=self.sems.at[2 * sem], recv_sem=self.sems.at[2 * sem + 1],
            device_id={"grp": to}, device_id_type=MESH,
        )

    def cut(self, ref, start, size):
        return ref.at[pl.ds(start, size), pl.ds(0, self.width)]

    def other(self, step):
        return lax.rem(self.chip + step, NCHIP)

    def first(self):
        half = self.rows // 2
        return self.copy(
            self.cut(self.src[0], self.src[1] + (1 - self.core) * half, half), self.cut(self.pre, 0, half), 0, self.partner
        )

    def second(self, step):
        size = self.rows // 8
        to = self.other(step)
        return self.copy(
            self.cut(self.cand, to * size, size),
            self.part.at[step - 1, :, pl.ds(0, self.width)], step, 2 * to + self.core,
        )

    def third(self, step):
        size = self.rows // 8
        at = self.base + self.core * (self.rows // 2) + self.chip * size
        return self.copy(
            self.cut(self.full, at, size), self.cut(self.full, at, size), NCHIP - 1 + step, 2 * self.other(step) + self.core
        )

    def fourth(self):
        half = self.rows // 2
        at = self.base + self.core * half
        return self.copy(self.cut(self.full, at, half), self.cut(self.full, at, half), 2 * NCHIP - 1, self.partner)

    def pairs(self):
        self.first().start()

    def scatter(self):
        self.first().wait_recv()
        half, cols = self.rows // 2, pl.ds(0, self.width)
        own = self.src[0][pl.ds(self.src[1] + self.core * half, half), cols]
        self.cand[:, cols] = jnp.where(self.own_me, own, self.pre[:, cols])
        for step in range(1, NCHIP):
            self.second(step).start()

    def collect(self):
        size, cols = self.rows // 8, pl.ds(0, self.width)
        value = self.cand[pl.ds(self.chip * size, size), cols]
        for step in range(1, NCHIP):
            self.second(step).wait_recv()
            value = jnp.where(self.shift == step, self.part[step - 1, :, cols], value)
        self.full[pl.ds(self.base + self.core * (self.rows // 2) + self.chip * size, size), cols] = value
        for step in range(1, NCHIP):
            self.third(step).start()

    def back(self):
        for step in range(1, NCHIP):
            self.third(step).wait_recv()
        self.fourth().start()

    def end(self):
        self.fourth().wait_recv()

    def sent(self):
        self.first().wait_send()
        self.fourth().wait_send()
        for step in range(1, NCHIP):
            self.second(step).wait_send()
            self.third(step).wait_send()


def gather_kernel(
    front_ref, blocks_ref, rows_ref, dest_ref, owner_ref,
    panel_out, trail_out, win_out, w_out, sym_out,
    part, trail, rowbuf, send_p, send_t, send_i, got_p, got_t, got_i,
    table, symm, diag, high_t, low_t, win_pre, win_cand, win_part, win_full, w_pre, w_cand, w_part, w_full,
    load_sem, own_sem, xs_sem, xr_sem, win_sem, w_sem, out_sem,
):
    front = lax.axis_index("front")
    group = lax.axis_index("grp")
    chip, core = group // 2, group % 2
    x, z = front // 4, front % 4
    rest = PB + WIN
    total = front_ref.shape[1]

    loads = [
        pltpu.make_async_copy(front_ref.at[0, pl.ds(0, total), pl.ds(0, PB)], part, load_sem.at[0]),
        pltpu.make_async_copy(front_ref.at[0, pl.ds(0, total), pl.ds(PB, WIN)], trail, load_sem.at[1]),
    ]
    loads[0].start()

    barrier = pltpu.get_barrier_semaphore()

    def after_me(hop):
        return lax.rem(x + hop[0], 4) * 4 + lax.rem(z + hop[1], 4)

    def before_me(hop):
        return lax.rem(x + 4 - hop[0], 4) * 4 + lax.rem(z + 4 - hop[1], 4)

    for hop in HOPS:
        pl.semaphore_signal(barrier, inc=1, device_id={"front": after_me(hop)}, device_id_type=MESH)
    partner = 2 * chip + (1 - core)
    pl.semaphore_signal(barrier, inc=1, device_id={"grp": partner}, device_id_type=MESH)
    for step in range(1, NCHIP):
        there = 2 * lax.rem(chip + step, NCHIP) + core
        pl.semaphore_signal(barrier, inc=1, device_id={"grp": there}, device_id_type=MESH)

    rowbuf[...] = jnp.zeros_like(rowbuf)
    rowbuf[0:KB, 0:BR] = rows_ref[...]
    spread = rowbuf[...]
    for width in (16, 32, 64):
        spread = spread + pltpu.roll(spread, width, 1)
    rowbuf[...] = spread
    dests = [dest_ref[k] for k in range(KB)]
    ranks = []
    for k in range(KB):
        rank = jnp.int32(0)
        for e in range(k):
            rank = rank + (dests[e] == dests[k]).astype(jnp.int32)
        ranks.append(rank)
    lane = lax.broadcasted_iota(jnp.int32, (8, 128), 1)
    mine = lax.rem(front, 4) * SLOT

    def choose(to, slot):
        pick, found = jnp.int32(0), jnp.int32(0)
        for k in range(KB):
            hit = ((dests[k] == to) & (ranks[k] == slot)).astype(jnp.int32)
            pick = pick + hit * k
            found = found + hit
        return pick, found

    def pack_panel(to, carry):
        index = jnp.zeros((8, 128), jnp.int32)
        for slot in range(CAP):
            pick, found = choose(to, slot)
            send_p[to, slot * BR : (slot + 1) * BR, :] = blocks_ref[pick, :, 0:PB]
            at = jnp.broadcast_to(rowbuf[pl.ds(pick, 1), :], (8, 128))
            at = jnp.where(found > 0, at, -1)
            base = mine + slot * BR
            index = jnp.where((lane >= base) & (lane < base + BR), at, index)
        send_i[to] = index
        return carry

    lax.fori_loop(0, NFRONT, pack_panel, 0)
    pl.semaphore_wait(barrier, NFRONT - 1 + 1 + NCHIP - 1)

    def exchange(src, dst, kind, n):
        to = after_me(HOPS[n])
        return pltpu.make_async_remote_copy(
            src_ref=src.at[to], dst_ref=dst.at[front],
            send_sem=xs_sem.at[kind, n], recv_sem=xr_sem.at[kind, n],
            device_id={"front": to}, device_id_type=MESH,
        )

    def arrival(src, dst, kind, n):
        came = before_me(HOPS[n])
        return pltpu.make_async_remote_copy(
            src_ref=src.at[came], dst_ref=dst.at[came],
            send_sem=xs_sem.at[kind, n], recv_sem=xr_sem.at[kind, n],
            device_id={"front": came}, device_id_type=MESH,
        )

    for n in range(NFRONT - 1):
        exchange(send_i, got_i, 0, n).start()
        exchange(send_p, got_p, 1, n).start()
    owns = [
        pltpu.make_async_copy(send_i.at[front], got_i.at[front], own_sem.at[0]),
        pltpu.make_async_copy(send_p.at[front], got_p.at[front], own_sem.at[1]),
        pltpu.make_async_copy(send_t.at[front], got_t.at[front], own_sem.at[2]),
    ]
    owns[0].start()
    owns[1].start()
    loads[1].start()

    def pack_trail(to, carry):
        for slot in range(CAP):
            pick, _ = choose(to, slot)
            send_t[to, slot * BR : (slot + 1) * BR, :] = blocks_ref[pick, :, PB:]
        return carry

    lax.fori_loop(0, NFRONT, pack_trail, 0)
    for n in range(NFRONT - 1):
        exchange(send_t, got_t, 2, n).start()
    owns[2].start()

    loads[0].wait()
    owns[0].wait()
    owns[1].wait()
    for n in range(NFRONT - 1):
        arrival(send_i, got_i, 0, n).wait_recv()
        arrival(send_p, got_p, 1, n).wait_recv()

    pieces = []
    for q in range(NFRONT // 4):
        piece = got_i[4 * q, 0:1, :]
        for s in range(1, 4):
            piece = piece + got_i[4 * q + s, 0:1, :]
        pieces.append(piece)
    index = jnp.concatenate(pieces, axis=1)
    high, low = split(got_p[...].reshape(KALL, PB))
    high, low = high.astype(BF16), low.astype(BF16)

    def onehot(base, size):
        at = lax.broadcasted_iota(jnp.int32, (size, KALL), 0) + base
        return jnp.where(at == index, 1.0, 0.0).astype(BF16)

    def assemble(tile, carry):
        base = pl.multiple_of(tile * TILE_A, TILE_A)
        at = onehot(base, TILE_A)
        part[pl.ds(base, TILE_A), :] = part[pl.ds(base, TILE_A), :] + (dot(at, high, NN) + dot(at, low, NN))
        return carry

    lax.fori_loop(0, total // TILE_A, assemble, 0)
    outs = [pltpu.make_async_copy(part, panel_out, out_sem.at[0])]
    outs[0].start()

    owner = owner_ref[0]
    ids = (chip, core, partner)
    flags = (owner == group, lax.rem(chip - owner // 2 + NCHIP, NCHIP))
    size = WIN // HALVES
    window = [
        Spread(ids, flags, (part, PB + h * size), win_full, h * size, size, PB,
               win_pre.at[h], win_cand.at[h], win_part.at[h], win_sem.at[h])
        for h in range(HALVES)
    ]
    inverse_rows = [
        Spread(ids, flags, (table, k * NB), w_full, k * NB, NB, NB * (k + 1),
               w_pre.at[k], w_cand.at[k], w_part.at[k], w_sem.at[k])
        for k in range(STEPS)
    ]
    for one in window:
        one.pairs()

    pivot = part[0:PB, :]
    sym = 0.5 * (pivot + pivot.T)
    symm[...] = sym
    table[...] = sym
    outs.append(pltpu.make_async_copy(symm, sym_out, out_sem.at[1]))
    outs[1].start()
    w_full[...] = jnp.zeros_like(w_full)

    plan = {
        (0, 0): [window[0].scatter],
        (0, 1): [window[1].scatter],
        (1, 2): [inverse_rows[0].scatter],
        (1, 3): [window[0].collect],
        (2, 1): [inverse_rows[0].collect],
        (2, 2): [inverse_rows[1].scatter],
        (2, 4): [window[1].collect],
        (3, 1): [inverse_rows[0].back],
        (3, 2): [inverse_rows[2].scatter],
        (3, 3): [inverse_rows[1].collect],
        (3, 5): [window[0].back],
    }

    wide = lax.broadcasted_iota(jnp.int32, (NB, PB), 1)
    for k in range(STEPS):
        base = k * NB
        diag[...] = table[base : base + NB, base : base + NB]
        for ib in range(NB // SB):
            eliminate(diag, ib)
            for task in plan.get((k, ib), ()):
                task()
        inverse = jnp.where(
            lax.broadcasted_iota(jnp.int32, (NB, NB), 0) >= lax.broadcasted_iota(jnp.int32, (NB, NB), 1),
            diag[...], 0.0,
        )
        above = table[base : base + NB, :]
        above = jnp.where((wide >= base) & (wide < base + NB), 0.0, above)
        reduced = dot3(inverse, above, NN)
        table[base : base + NB, :] = reduced
        table[base : base + NB, base : base + NB] = inverse
        inverse_rows[k].pairs()
        if k + 1 < STEPS:
            upper = table[base : base + NB, :]
            left = reduced[:, base + NB :]
            update = dot3(left, upper, TN)
            old = table[base + NB :, :]
            col = lax.broadcasted_iota(jnp.int32, old.shape, 1)
            old = jnp.where((col >= base) & (col < base + NB), 0.0, old)
            table[base + NB :, :] = old - update

    inverse_rows[3].scatter()
    inverse_rows[2].collect()
    inverse_rows[1].back()

    loads[1].wait()
    owns[2].wait()
    for n in range(NFRONT - 1):
        arrival(send_t, got_t, 2, n).wait_recv()
    head, tail = split(got_t[...].reshape(KALL, WIN))
    high_t[...] = head.astype(BF16)
    low_t[...] = tail.astype(BF16)

    def add_trail(tile, carry):
        base = pl.multiple_of(tile * TILE_A, TILE_A)
        at = onehot(base, TILE_A)
        trail[pl.ds(base, TILE_A), :] = trail[pl.ds(base, TILE_A), :] + (
            dot(at, high_t[...], NN) + dot(at, low_t[...], NN)
        )
        return carry

    tiles = total // TILE_A
    cuts = [0, 3 * tiles // 8, 6 * tiles // 8, tiles]
    tasks = [
        [inverse_rows[3].collect, inverse_rows[2].back],
        [window[1].back, inverse_rows[3].back],
        [],
    ]
    for part_at in range(3):
        lax.fori_loop(cuts[part_at], cuts[part_at + 1], add_trail, 0)
        rows = pl.ds(cuts[part_at] * TILE_A, (cuts[part_at + 1] - cuts[part_at]) * TILE_A)
        outs.append(pltpu.make_async_copy(trail.at[rows, :], trail_out.at[rows, :], out_sem.at[2 + part_at]))
        outs[-1].start()
        for task in tasks[part_at]:
            task()

    for one in window:
        one.end()
    outs.append(pltpu.make_async_copy(win_full, win_out, out_sem.at[5]))
    outs[-1].start()
    for one in inverse_rows:
        one.end()
    outs.append(pltpu.make_async_copy(w_full, w_out, out_sem.at[6]))
    outs[-1].start()

    for n in range(NFRONT - 1):
        exchange(send_i, got_i, 0, n).wait_send()
        exchange(send_p, got_p, 1, n).wait_send()
        exchange(send_t, got_t, 2, n).wait_send()
    for one in window + inverse_rows:
        one.sent()
    for one in outs:
        one.wait()


def gather(front_block, blocks, rows, dest, owner):
    vmem = pl.BlockSpec(memory_space=pltpu.VMEM)
    smem = pl.BlockSpec(memory_space=pltpu.SMEM)
    hbm = pl.BlockSpec(memory_space=pl.ANY)
    dma = pltpu.SemaphoreType.DMA
    total = front_block.shape[1]
    size = WIN // HALVES

    def buf(*shape, dtype=F32):
        return pltpu.VMEM(shape, dtype)

    return pl.pallas_call(
        gather_kernel,
        out_shape=[
            jax.ShapeDtypeStruct((total, PB), F32),
            jax.ShapeDtypeStruct((total, WIN), F32),
            jax.ShapeDtypeStruct((WIN, PB), F32),
            jax.ShapeDtypeStruct((PB, PB), F32),
            jax.ShapeDtypeStruct((PB, PB), F32),
        ],
        in_specs=[hbm, vmem, vmem, smem, smem],
        out_specs=[hbm] * 5,
        scratch_shapes=[
            buf(total, PB), buf(total, WIN), buf(8, 128, dtype=jnp.int32),
            buf(NFRONT, SLOT, PB), buf(NFRONT, SLOT, WIN), buf(NFRONT, 8, 128, dtype=jnp.int32),
            buf(NFRONT, SLOT, PB), buf(NFRONT, SLOT, WIN), buf(NFRONT, 8, 128, dtype=jnp.int32),
            buf(PB, PB), buf(PB, PB), buf(NB, NB),
            buf(KALL, WIN, dtype=BF16), buf(KALL, WIN, dtype=BF16),
            buf(HALVES, size // 2, PB), buf(HALVES, size // 2, PB),
            buf(HALVES, NCHIP - 1, size // 8, PB), buf(WIN, PB),
            buf(STEPS, NB // 2, PB), buf(STEPS, NB // 2, PB),
            buf(STEPS, NCHIP - 1, NB // 8, PB), buf(PB, PB),
            dma((2,)), dma((3,)), dma((3, NFRONT)), dma((3, NFRONT)),
            dma((HALVES, 4 * NCHIP)), dma((STEPS, 4 * NCHIP)), dma((7,)),
        ],
        compiler_params=pltpu.CompilerParams(
            collective_id=0, has_side_effects=True, vmem_limit_bytes=56 * 2**20
        ),
        name="gather",
    )(front_block, blocks, rows, dest, owner)


TILE = 512


def finish_kernel(owner_ref, a_ref, b_ref, w_ref, win_ref, sym_ref, panel_ref, schur_ref, wh, wl, vh, vl):
    step = pl.program_id(0)

    def solve(left):
        lh, ll = split(left)
        lh, ll = lh.astype(BF16), ll.astype(BF16)
        half = PB // 2
        sides = []
        for n, depth in ((0, half), (half, PB)):
            ah, al = lh[:, :depth], ll[:, :depth]
            bh, bl = wh[n : n + half, :depth], wl[n : n + half, :depth]
            sides.append(dot(ah, bh, NT) + (dot(ah, bl, NT) + dot(al, bh, NT)))
        return jnp.concatenate(sides, axis=1)

    @pl.when(step == 0)
    def _():
        high, low = split(w_ref[...])
        wh[...] = high.astype(BF16)
        wl[...] = low.astype(BF16)
        for base in range(0, WIN, 128):
            high, low = split(solve(win_ref[base : base + 128, :]))
            vh[base : base + 128, :] = high.astype(BF16)
            vl[base : base + 128, :] = low.astype(BF16)

    solved = solve(a_ref[...])
    panel_ref[0] = solved
    sh, sl = split(solved)
    product = dot(sh, vh[...], NT) + (dot(sh, vl[...], NT) + dot(sl, vh[...], NT))
    schur_ref[0] = b_ref[...] - product

    @pl.when((step < PB // TILE) & (owner_ref[0] == owner_ref[1]))
    def _():
        top = pl.multiple_of(step * TILE, TILE)
        factor = solve(sym_ref[pl.ds(top, TILE), :])
        row = lax.broadcasted_iota(jnp.int32, (TILE, PB), 0) + top
        panel_ref[0] = jnp.where(row >= lax.broadcasted_iota(jnp.int32, (TILE, PB), 1), factor, 0.0)


def finish(owner2, a, b, w, window, sym):
    rows = a.shape[0]
    smem = pl.BlockSpec(memory_space=pltpu.SMEM)

    def whole(v):
        return pl.BlockSpec(v.shape, lambda i: (0, 0), pipeline_mode=pl.Buffered(1))

    return pl.pallas_call(
        finish_kernel,
        grid=(rows // TILE,),
        out_shape=[jax.ShapeDtypeStruct((1, rows, PB), F32), jax.ShapeDtypeStruct((1, rows, WIN), F32)],
        in_specs=[smem, pl.BlockSpec((TILE, PB), lambda i: (i, 0)), pl.BlockSpec((TILE, WIN), lambda i: (i, 0))]
        + [whole(v) for v in (w, window, sym)],
        out_specs=[
            pl.BlockSpec((1, TILE, PB), lambda i: (0, i, 0)),
            pl.BlockSpec((1, TILE, WIN), lambda i: (0, i, 0)),
        ],
        scratch_shapes=[
            pltpu.VMEM((PB, PB), BF16), pltpu.VMEM((PB, PB), BF16),
            pltpu.VMEM((WIN, PB), BF16), pltpu.VMEM((WIN, PB), BF16),
        ],
        compiler_params=pltpu.CompilerParams(vmem_limit_bytes=56 * 2**20),
        name="finish",
    )(owner2, a, b, w, window, sym)


def local(front_block, child_blocks, child_rows, child_dest, panel_owner):
    panel, trail, window, w, sym = gather(
        front_block, child_blocks[0, 0], child_rows[0, 0], child_dest.reshape(KB), panel_owner
    )
    owner2 = jnp.concatenate([panel_owner, lax.axis_index("grp").astype(jnp.int32)[None]])
    return tuple(finish(owner2, panel, trail, w, window, sym))


def solution(mesh):
    placed = (
        P("front", "grp", None),
        P("front", "grp", None, None, None),
        P("front", "grp", None, None),
        P("front", "grp", None, None),
        P("front"),
    )
    return jax.shard_map(
        local,
        mesh=mesh,
        in_specs=placed,
        out_specs=(P("front", "grp", None), P("front", "grp", None)),
        check_vma=False,
    )
```

time: 412 us -> 108 us (0.26); the launches traced: 406 us -> 107 us
  waiting for transfers between devices: 156 us -> 0 us
  other arithmetic: 142 us -> 0.6 us
  Pallas kernels: 0 us -> 105 us
  matrix products: 40.4 us -> 0 us
  local copies, waits for them, and re-layouts: 37.6 us -> 0 us
  between operations: 17.9 us -> 1.29 us
  starting transfers between devices: 12 us -> 0 us
    another operation x18 -> x0, other arithmetic: 121 us -> none  [the longest x14 79.1 us: local(): pivot_factor = jnp.linalg.cholesky(symmetric)]
    psum x2 -> x0, waiting for transfers between devices: 114 us -> none  [spread(): return lax.psum(jnp.where(mine, array, jnp.zeros_like(array)), axis)]
    pallas_call x0 -> x2, Pallas kernels: none -> 105 us  [the longest x1 82.4 us: gather(): pl.pallas_call(gather_kernel, out_shape=[jax.ShapeDtypeStruct((total, PB)...]
    all_to_all x2 -> x0, waiting for transfers between devices: 41.9 us -> none  [the longest x1 38.4 us: local(): lax.all_to_all(send_blocks, 'front', split_axis=0, concat_axis=0, tiled=T...]
    another operation x13 -> x0, matrix products: 22.8 us -> none  [the longest x7 20.5 us: right_solve(): lax.linalg.triangular_solve(factor, rows, left_side=False, lower=True, tr...]
    dot_general x1 -> x0, matrix products: 17.7 us -> none  [local(): jnp.dot(solved, window.T, precision=lax.Precision.HIGHEST)]
    unnamed x21 -> x0, local copies, waits for them, and re-layouts: 17.4 us -> none
    scatter-add x1 -> x0, other arithmetic: 14 us -> none  [local(): local_rows.at[flat_rows].add(got_blocks.reshape(-1, local_rows.shape[1]))]
  transfers between devices with their start and end apart: 4 -> 0, of which waited for: 4 -> 0; matrix products, arithmetic and copies ran while one was open for 3% -> 0% of each run, Pallas kernels for 0% -> 0%
where the time goes in v2:
time: 108 us; the launch traced here: 107 us
  Pallas kernels  105 us (97%)
  between operations  1.29 us (1%)
    pallas_call x1, Pallas kernels, gather(): pl.pallas_call(gather_kernel, out_shape=[jax.ShapeDtypeStruct((total, PB)...  82.4 us
    pallas_call x1, Pallas kernels, finish(): pl.pallas_call(finish_kernel, grid=(rows // TILE,), out_shape=[jax.ShapeD...  22.3 us

profile of v2, /device:TPU:0, one launch (start us, length us, event | category | flops | bytes accessed | tf_op | source)
XLA Modules:
  0.0 106.5 jit_solution(2129106980040412447)
XLA Ops:
  1.3 0.6 pad_add_fusion.owner_ref
  1.9 82.4 %gather.1 = (f32[2048,512]{1,0:T(8,128)}, f32[2048,896]{1,0:T(8,128)}, f32[896,512]{1,0:T(8,128)}, f32[512,512]{1,0:T(8,128)}, f32[512,512]{1,0:T(8,128)}) custom-call(f32[1,2048,1408]{2,1,0:T(8,128)} %front_ref.1, f32[4,16,1408]{2,1,0:T(8,128)} %bitcast.4, s32[4,16]{1,0:T(4,128)} %bitcast.5, s32[4]{0:T(128)} %bitcast.6, s32[1]{0:T(128)S(6)} %copy.7.owner_ref), custom_call_target="tpu_custom_call" | custom-call | tf_op jit(solution)/shard_map/gather/pallas_call | solution.py:439
  84.3 22.3 %finish.1 = (f32[1,2048,512]{2,1,0:T(8,128)}, f32[1,2048,896]{2,1,0:T(8,128)}) custom-call(s32[2]{0:T(128)} %pad_add_fusion.owner_ref, f32[2048,512]{1,0:T(8,128)} %get-tuple-element.7.a_ref, f32[2048,896]{1,0:T(8,128)} %get-tuple-element.8.b_ref, f32[512,512]{1,0:T(8,128)} %get-tuple-element.9.w_ref, f32[896,512]{1,0:T(8,128)} %get-tuple-element.10.win_ref, ...), custom_call_target="tpu_custom_call" | custom-call | tf_op jit(solution)/shard_map/finish/pallas_call | solution.py:518

commit v3 on v2

--- a/solution.py
+++ b/solution.py
@@ -76,6 +76,7 @@
 HOPS = [(dx, dz) for dx in range(4) for dz in range(4)][1:]
 HOPS.sort(key=lambda p: -(min(p[0], 4 - p[0]) + min(p[1], 4 - p[1])))
 TILE_A = 256
+FIRST, EVERY = 1, 2
 
 
 class Spread:
@@ -270,8 +271,6 @@
         return carry
 
     lax.fori_loop(0, NFRONT, pack_trail, 0)
-    for n in range(NFRONT - 1):
-        exchange(send_t, got_t, 2, n).start()
     owns[2].start()
 
     loads[0].wait()
@@ -302,8 +301,10 @@
         return carry
 
     lax.fori_loop(0, total // TILE_A, assemble, 0)
-    outs = [pltpu.make_async_copy(part, panel_out, out_sem.at[0])]
-    outs[0].start()
+    outs = [
+        pltpu.make_async_copy(part, panel_out, out_sem.at[0]),
+        pltpu.make_async_copy(symm, sym_out, out_sem.at[1]),
+    ]
 
     owner = owner_ref[0]
     ids = (chip, core, partner)
@@ -326,23 +327,28 @@
     sym = 0.5 * (pivot + pivot.T)
     symm[...] = sym
     table[...] = sym
-    outs.append(pltpu.make_async_copy(symm, sym_out, out_sem.at[1]))
-    outs[1].start()
     w_full[...] = jnp.zeros_like(w_full)
 
     plan = {
-        (0, 0): [window[0].scatter],
-        (0, 1): [window[1].scatter],
+        (0, 1): [window[0].scatter],
+        (0, 3): [window[1].scatter],
+        (0, 6): [outs[1].start],
+        (1, 0): [outs[0].start],
         (1, 2): [inverse_rows[0].scatter],
-        (1, 3): [window[0].collect],
-        (2, 1): [inverse_rows[0].collect],
+        (1, 4): [window[0].collect],
+        (1, 6): [inverse_rows[0].collect],
+        (2, 1): [inverse_rows[0].back],
         (2, 2): [inverse_rows[1].scatter],
-        (2, 4): [window[1].collect],
-        (3, 1): [inverse_rows[0].back],
+        (2, 5): [window[1].collect],
+        (2, 6): [inverse_rows[1].collect],
+        (3, 0): [window[0].back],
+        (3, 1): [inverse_rows[1].back],
         (3, 2): [inverse_rows[2].scatter],
-        (3, 3): [inverse_rows[1].collect],
-        (3, 5): [window[0].back],
+        (3, 6): [inverse_rows[2].collect],
     }
+    for n in range(NFRONT - 1):
+        at = FIRST + EVERY * n
+        plan.setdefault((at // (NB // SB), at % (NB // SB)), []).append(exchange(send_t, got_t, 2, n).start)
 
     wide = lax.broadcasted_iota(jnp.int32, (NB, PB), 1)
     for k in range(STEPS):
@@ -372,8 +378,7 @@
             table[base + NB :, :] = old - update
 
     inverse_rows[3].scatter()
-    inverse_rows[2].collect()
-    inverse_rows[1].back()
+    inverse_rows[2].back()
 
     loads[1].wait()
     owns[2].wait()
@@ -393,11 +398,7 @@
 
     tiles = total // TILE_A
     cuts = [0, 3 * tiles // 8, 6 * tiles // 8, tiles]
-    tasks = [
-        [inverse_rows[3].collect, inverse_rows[2].back],
-        [window[1].back, inverse_rows[3].back],
-        [],
-    ]
+    tasks = [[inverse_rows[3].collect, window[1].back], [inverse_rows[3].back], []]
     for part_at in range(3):
         lax.fori_loop(cuts[part_at], cuts[part_at + 1], add_trail, 0)
         rows = pl.ds(cuts[part_at] * TILE_A, (cuts[part_at + 1] - cuts[part_at]) * TILE_A)
@@ -470,34 +471,32 @@
 TILE = 512
 
 
-def finish_kernel(owner_ref, a_ref, b_ref, w_ref, win_ref, sym_ref, panel_ref, schur_ref, wh, wl, vh, vl):
+def finish_kernel(owner_ref, a_ref, b_ref, w_ref, win_ref, sym_ref, panel_ref, schur_ref, wa, wb, vv):
     step = pl.program_id(0)
 
     def solve(left):
         lh, ll = split(left)
         lh, ll = lh.astype(BF16), ll.astype(BF16)
         half = PB // 2
-        sides = []
-        for n, depth in ((0, half), (half, PB)):
-            ah, al = lh[:, :depth], ll[:, :depth]
-            bh, bl = wh[n : n + half, :depth], wl[n : n + half, :depth]
-            sides.append(dot(ah, bh, NT) + (dot(ah, bl, NT) + dot(al, bh, NT)))
-        return jnp.concatenate(sides, axis=1)
+        near = jnp.concatenate([lh[:, :half], lh[:, :half], ll[:, :half]], axis=1)
+        return jnp.concatenate([dot(near, wa[...], NT), dot(jnp.concatenate([lh, lh, ll], axis=1), wb[...], NT)], axis=1)
 
     @pl.when(step == 0)
     def _():
         high, low = split(w_ref[...])
-        wh[...] = high.astype(BF16)
-        wl[...] = low.astype(BF16)
-        for base in range(0, WIN, 128):
-            high, low = split(solve(win_ref[base : base + 128, :]))
-            vh[base : base + 128, :] = high.astype(BF16)
-            vl[base : base + 128, :] = low.astype(BF16)
+        high, low = high.astype(BF16), low.astype(BF16)
+        half = PB // 2
+        wa[...] = jnp.concatenate([high[:half, :half], low[:half, :half], high[:half, :half]], axis=1)
+        wb[...] = jnp.concatenate([high[half:], low[half:], high[half:]], axis=1)
+        high, low = split(solve(win_ref[...]))
+        high, low = high.astype(BF16), low.astype(BF16)
+        vv[...] = jnp.concatenate([high, low, high], axis=1)
 
     solved = solve(a_ref[...])
     panel_ref[0] = solved
     sh, sl = split(solved)
-    product = dot(sh, vh[...], NT) + (dot(sh, vl[...], NT) + dot(sl, vh[...], NT))
+    sh, sl = sh.astype(BF16), sl.astype(BF16)
+    product = dot(jnp.concatenate([sh, sh, sl], axis=1), vv[...], NT)
     schur_ref[0] = b_ref[...] - product
 
     @pl.when((step < PB // TILE) & (owner_ref[0] == owner_ref[1]))
@@ -526,8 +525,8 @@
             pl.BlockSpec((1, TILE, WIN), lambda i: (0, i, 0)),
         ],
         scratch_shapes=[
-            pltpu.VMEM((PB, PB), BF16), pltpu.VMEM((PB, PB), BF16),
-            pltpu.VMEM((WIN, PB), BF16), pltpu.VMEM((WIN, PB), BF16),
+            pltpu.VMEM((PB // 2, 3 * PB // 2), BF16), pltpu.VMEM((PB // 2, 3 * PB), BF16),
+            pltpu.VMEM((WIN, 3 * PB), BF16),
         ],
         compiler_params=pltpu.CompilerParams(vmem_limit_bytes=56 * 2**20),
         name="finish",

time: 108 us -> 95.6 us (0.89); the launches traced: 107 us -> 95.4 us
  Pallas kernels: 105 us -> 93.5 us
    pallas_call x1, Pallas kernels: 22.3 us -> 16.4 us  [finish(): pl.pallas_call(finish_kernel, grid=(rows // TILE,), out_shape=[jax.ShapeD...]
    pallas_call x1, Pallas kernels: 82.4 us -> 77.1 us  [gather(): pl.pallas_call(gather_kernel, out_shape=[jax.ShapeDtypeStruct((total, PB)...]
where the time goes in v3:
time: 95.6 us; the launch traced here: 95.4 us
  Pallas kernels  93.5 us (98%)
  between operations  1.29 us (1%)
    pallas_call x1, Pallas kernels, gather(): pl.pallas_call(gather_kernel, out_shape=[jax.ShapeDtypeStruct((total, PB)...  77.1 us
    pallas_call x1, Pallas kernels, finish(): pl.pallas_call(finish_kernel, grid=(rows // TILE,), out_shape=[jax.ShapeD...  16.4 us

profile of v3, /device:TPU:0, one launch (start us, length us, event | category | flops | bytes accessed | tf_op | source)
XLA Modules:
  0.0 95.4 jit_solution(15444222216450940928)
XLA Ops:
  1.3 0.6 pad_add_fusion.owner_ref
  1.9 77.1 %gather.1 = (f32[2048,512]{1,0:T(8,128)}, f32[2048,896]{1,0:T(8,128)}, f32[896,512]{1,0:T(8,128)}, f32[512,512]{1,0:T(8,128)}, f32[512,512]{1,0:T(8,128)}) custom-call(f32[1,2048,1408]{2,1,0:T(8,128)} %front_ref.1, f32[4,16,1408]{2,1,0:T(8,128)} %bitcast.4, s32[4,16]{1,0:T(4,128)} %bitcast.5, s32[4]{0:T(128)} %bitcast.6, s32[1]{0:T(128)S(6)} %copy.7.owner_ref), custom_call_target="tpu_custom_call" | custom-call | tf_op jit(solution)/shard_map/gather/pallas_call | solution.py:440
  79.0 16.4 %finish.1 = (f32[1,2048,512]{2,1,0:T(8,128)}, f32[1,2048,896]{2,1,0:T(8,128)}) custom-call(s32[2]{0:T(128)} %pad_add_fusion.owner_ref, f32[2048,512]{1,0:T(8,128)} %get-tuple-element.7.a_ref, f32[2048,896]{1,0:T(8,128)} %get-tuple-element.8.b_ref, f32[512,512]{1,0:T(8,128)} %get-tuple-element.9.w_ref, f32[896,512]{1,0:T(8,128)} %get-tuple-element.10.win_ref, ...), custom_call_target="tpu_custom_call" | custom-call | tf_op jit(solution)/shard_map/finish/pallas_call | solution.py:517

commit v4 on v3

--- a/solution.py
+++ b/solution.py
@@ -76,7 +76,7 @@
 HOPS = [(dx, dz) for dx in range(4) for dz in range(4)][1:]
 HOPS.sort(key=lambda p: -(min(p[0], 4 - p[0]) + min(p[1], 4 - p[1])))
 TILE_A = 256
-FIRST, EVERY = 1, 2
+FIRST, EVERY = 4, 1
 
 
 class Spread:
@@ -300,7 +300,8 @@
         part[pl.ds(base, TILE_A), :] = part[pl.ds(base, TILE_A), :] + (dot(at, high, NN) + dot(at, low, NN))
         return carry
 
-    lax.fori_loop(0, total // TILE_A, assemble, 0)
+    near = -(-rest // TILE_A)
+    lax.fori_loop(0, near, assemble, 0)
     outs = [
         pltpu.make_async_copy(part, panel_out, out_sem.at[0]),
         pltpu.make_async_copy(symm, sym_out, out_sem.at[1]),
@@ -330,20 +331,20 @@
     w_full[...] = jnp.zeros_like(w_full)
 
     plan = {
-        (0, 1): [window[0].scatter],
-        (0, 3): [window[1].scatter],
+        (0, 0): [window[0].scatter],
+        (0, 2): [window[1].scatter],
         (0, 6): [outs[1].start],
-        (1, 0): [outs[0].start],
-        (1, 2): [inverse_rows[0].scatter],
-        (1, 4): [window[0].collect],
-        (1, 6): [inverse_rows[0].collect],
-        (2, 1): [inverse_rows[0].back],
-        (2, 2): [inverse_rows[1].scatter],
-        (2, 5): [window[1].collect],
-        (2, 6): [inverse_rows[1].collect],
-        (3, 0): [window[0].back],
-        (3, 1): [inverse_rows[1].back],
+        (1, 2): [window[0].collect],
+        (1, 3): [inverse_rows[0].scatter],
+        (2, 1): [window[1].collect],
+        (2, 2): [inverse_rows[0].collect],
+        (2, 3): [inverse_rows[1].scatter],
+        (2, 5): [window[0].back],
+        (2, 7): [inverse_rows[1].collect],
+        (3, 0): [inverse_rows[0].back],
         (3, 2): [inverse_rows[2].scatter],
+        (3, 4): [window[1].back],
+        (3, 5): [inverse_rows[1].back],
         (3, 6): [inverse_rows[2].collect],
     }
     for n in range(NFRONT - 1):
@@ -379,6 +380,8 @@
 
     inverse_rows[3].scatter()
     inverse_rows[2].back()
+    lax.fori_loop(near, total // TILE_A, assemble, 0)
+    outs[0].start()
 
     loads[1].wait()
     owns[2].wait()
@@ -398,7 +401,7 @@
 
     tiles = total // TILE_A
     cuts = [0, 3 * tiles // 8, 6 * tiles // 8, tiles]
-    tasks = [[inverse_rows[3].collect, window[1].back], [inverse_rows[3].back], []]
+    tasks = [[inverse_rows[3].collect], [inverse_rows[3].back], []]
     for part_at in range(3):
         lax.fori_loop(cuts[part_at], cuts[part_at + 1], add_trail, 0)
         rows = pl.ds(cuts[part_at] * TILE_A, (cuts[part_at + 1] - cuts[part_at]) * TILE_A)
@@ -499,7 +502,7 @@
     product = dot(jnp.concatenate([sh, sh, sl], axis=1), vv[...], NT)
     schur_ref[0] = b_ref[...] - product
 
-    @pl.when((step < PB // TILE) & (owner_ref[0] == owner_ref[1]))
+    @pl.when((step < PB // TILE) & (owner_ref[0] == lax.axis_index("grp")))
     def _():
         top = pl.multiple_of(step * TILE, TILE)
         factor = solve(sym_ref[pl.ds(top, TILE), :])
@@ -507,7 +510,7 @@
         panel_ref[0] = jnp.where(row >= lax.broadcasted_iota(jnp.int32, (TILE, PB), 1), factor, 0.0)
 
 
-def finish(owner2, a, b, w, window, sym):
+def finish(owner, a, b, w, window, sym):
     rows = a.shape[0]
     smem = pl.BlockSpec(memory_space=pltpu.SMEM)
 
@@ -530,15 +533,14 @@
         ],
         compiler_params=pltpu.CompilerParams(vmem_limit_bytes=56 * 2**20),
         name="finish",
-    )(owner2, a, b, w, window, sym)
+    )(owner, a, b, w, window, sym)
 
 
 def local(front_block, child_blocks, child_rows, child_dest, panel_owner):
     panel, trail, window, w, sym = gather(
         front_block, child_blocks[0, 0], child_rows[0, 0], child_dest.reshape(KB), panel_owner
     )
-    owner2 = jnp.concatenate([panel_owner, lax.axis_index("grp").astype(jnp.int32)[None]])
-    return tuple(finish(owner2, panel, trail, w, window, sym))
+    return tuple(finish(panel_owner, panel, trail, w, window, sym))
 
 
 def solution(mesh):

time: 95.6 us -> 91.2 us (0.954)
  Pallas kernels: 93.5 us -> 89.7 us
    pallas_call x1, Pallas kernels: 77.1 us -> 73.4 us  [gather(): pl.pallas_call(gather_kernel, out_shape=[jax.ShapeDtypeStruct((total, PB)...]
where the time goes in v4:
time: 91.2 us; the launch traced here: 91 us
  Pallas kernels  89.7 us (98%)
  between operations  1.29 us (1%)
    pallas_call x1, Pallas kernels, gather(): pl.pallas_call(gather_kernel, out_shape=[jax.ShapeDtypeStruct((total, PB)...  73.4 us
    pallas_call x1, Pallas kernels, finish(): pl.pallas_call(finish_kernel, grid=(rows // TILE,), out_shape=[jax.ShapeD...  16.4 us

profile of v4, /device:TPU:0, one launch (start us, length us, event | category | flops | bytes accessed | tf_op | source)
XLA Modules:
  0.0 91.0 jit_solution(15925034809182912309)
XLA Ops:
  1.3 73.4 %gather.1 = (f32[2048,512]{1,0:T(8,128)}, f32[2048,896]{1,0:T(8,128)}, f32[896,512]{1,0:T(8,128)}, f32[512,512]{1,0:T(8,128)}, f32[512,512]{1,0:T(8,128)}) custom-call(f32[1,2048,1408]{2,1,0:T(8,128)} %front_ref.1, f32[4,16,1408]{2,1,0:T(8,128)} %bitcast.3, s32[4,16]{1,0:T(4,128)} %bitcast.4, s32[4]{0:T(128)} %bitcast.5, s32[1]{0:T(128)S(6)} %copy.7.owner_ref), custom_call_target="tpu_custom_call" | custom-call | tf_op jit(solution)/shard_map/gather/pallas_call | solution.py:443
  74.7 16.4 %finish.1 = (f32[1,2048,512]{2,1,0:T(8,128)}, f32[1,2048,896]{2,1,0:T(8,128)}) custom-call(s32[1]{0:T(128)S(6)} %copy.7.owner_ref, f32[2048,512]{1,0:T(8,128)} %get-tuple-element.7.a_ref, f32[2048,896]{1,0:T(8,128)} %get-tuple-element.8.b_ref, f32[512,512]{1,0:T(8,128)} %get-tuple-element.9.w_ref, f32[896,512]{1,0:T(8,128)} %get-tuple-element.10.win_ref, ...), custom_call_target="tpu_custom_call" | custom-call | tf_op jit(solution)/shard_map/finish/pallas_call | solution.py:520
